TPU v7x, 512 devices: a whole 4x8x8 slice. The times are simulated.
512 devices in a mesh: blk: 32 (over y, z_lo, core), grp: 16 (over z_hi, x).
Axes of the slice: x: 4, y: 8, z: 8 (z_hi: 4, z_lo: 2; z = z_hi * 2 + z_lo), core: 2. Of those that a mesh axis runs over, the one named last changes fastest.
Arguments:
- points: bfloat16 [16, 65536], P(None, ('blk', 'grp')), may hold values from -6 to 6, as said below
- right_side: float32 [64, 65536], P(None, ('blk', 'grp')), may hold values from -10 to 16
- nugget: float32 [65536], P(('blk', 'grp')), may hold values from 2 to 3
- scales: float32 [16], replicated, may hold values from 0.8 to 1.25
- pairs: int32 [32, 3], replicated, may hold values 0 or 1
Outputs:
- solution: float32 [64, 65536], P(None, ('blk', 'grp'))
- residual: float32 [64, 65536], P(None, ('blk', 'grp'))
Inputs may be any that keep to these rules, and one draw needn't show every extreme that they name: pairs[b, d - 1] is 1 when block b and block (b + d) mod 32 share a tile. In features 0 and 1 the points of block b lie on the circle of radius 32 / (2 pi) about the anchor, at arc lengths from b to b + 3 + 1 (measured round the circle from feature 1 = 0), one point in each of 2048 equal slots of that arc; features 2 to 15 lie between 0 and 0.3.
All inputs are finite; a program needn't handle non-finite values.
Results may differ from a plain program's by a relative error of at most 0.0006.
Values may be sent and summed in bfloat16 or wider, within the bound.
A program may use at most 64 MiB of HBM per device.

v0:
```python
import jax
import jax.numpy as jnp
from jax import lax
from jax.sharding import PartitionSpec as P

ITERS = 2


def passed_along(block, axis, distance):
    devices = range(lax.axis_size(axis))
    route = [((i - distance) % len(devices), i) for i in devices]
    return lax.ppermute(block, axis, route)


def kernel_tile(row_z, col_z):
    cross = jnp.dot(
        row_z.T, col_z, precision=lax.Precision.HIGHEST, preferred_element_type=jnp.float32
    )
    squared = (
        jnp.sum(row_z * row_z, axis=0)[:, None]
        + jnp.sum(col_z * col_z, axis=0)[None, :]
        - 2.0 * cross
    )
    distance = jnp.sqrt(jnp.maximum(squared, 0.0))
    spare = jnp.maximum(1.0 - distance, 0.0)
    return (spare**4 * (4.0 * distance + 1.0)).astype(jnp.bfloat16)


def tile_terms(row_z, row_vec, column_block, scales, transpose):
    feat = row_z.shape[0]
    col_z = column_block[:feat].astype(jnp.float32) / scales[:, None]
    col_vec = column_block[feat:]
    total = col_z.shape[1]
    width = min(512, total)
    count = total // width
    nrhs = col_vec.shape[0]
    rows = row_z.shape[1]

    def step(carry, index):
        ahead, behind = carry
        start = index * width
        part_z = lax.dynamic_slice_in_dim(col_z, start, width, 1)
        part_v = lax.dynamic_slice_in_dim(col_vec, start, width, 1)
        tile = kernel_tile(row_z, part_z)
        ahead = ahead + lax.dot_general(
            part_v, tile, (((1,), (1,)), ((), ())), preferred_element_type=jnp.float32
        )
        if transpose:
            piece = jnp.dot(row_vec, tile, preferred_element_type=jnp.float32)
            behind = lax.dynamic_update_slice_in_dim(behind, piece, start, 1)
        return ((ahead, behind), None)

    start_carry = (jnp.zeros((nrhs, rows), jnp.float32), jnp.zeros((nrhs, total), jnp.float32))
    result, unused = lax.scan(step, start_carry, jnp.arange(count, dtype=jnp.int32))
    return result


def on_device(points, right_side, nugget, scales, pairs):
    ngrp = lax.axis_size("grp")
    rows = points.shape[1]
    maxp = pairs.shape[1]
    nrhs = right_side.shape[0]
    total = rows * ngrp
    here = lax.axis_index("blk")
    amp = 1.0 / (total + 16)
    own_z = points.astype(jnp.float32) / scales[:, None]

    def squares(values):
        return lax.psum(jnp.sum(values * values, axis=1), ("blk", "grp"))

    solution = jnp.zeros(right_side.shape, jnp.float32)
    residual = right_side
    direction = right_side
    norm_now = squares(residual)
    for step in range(ITERS):
        rounded = direction.astype(jnp.bfloat16)
        stacked = jnp.concatenate([points, rounded], axis=0)
        own = lax.all_gather(stacked, "grp", axis=1, tiled=True)
        forward, unused = tile_terms(own_z, rounded, own, scales, False)
        incoming = jnp.zeros((nrhs, total), jnp.float32)
        for offset in range(1, maxp + 1):
            partner = passed_along(own, "blk", -offset)
            active = lax.dynamic_index_in_dim(pairs[:, offset - 1], here, keepdims=False) == 1
            column_block = partner
            ahead, behind = lax.cond(
                active,
                lambda: tile_terms(own_z, rounded, column_block, scales, True),
                lambda: (
                    jnp.zeros((nrhs, rows), jnp.float32),
                    jnp.zeros((nrhs, total), jnp.float32),
                ),
            )
            forward = forward + ahead
            incoming = incoming + passed_along(behind, "blk", offset)
        forward = forward + lax.psum_scatter(incoming, "grp", scatter_dimension=1, tiled=True)
        image = nugget[None, :] * direction + amp * forward
        alpha = norm_now / lax.psum(jnp.sum(direction * image, axis=1), ("blk", "grp"))
        solution = solution + alpha[:, None] * direction
        residual = residual - alpha[:, None] * image
        if step + 1 < ITERS:
            norm_next = squares(residual)
            direction = residual + (norm_next / norm_now)[:, None] * direction
            norm_now = norm_next
    return (solution, residual)


def solution(mesh):
    placed = (P(None, ("blk", "grp")), P(None, ("blk", "grp")), P(("blk", "grp")), P(), P())
    return jax.shard_map(
        on_device,
        mesh=mesh,
        in_specs=placed,
        out_specs=(P(None, ("blk", "grp")), P(None, ("blk", "grp"))),
        check_vma=False,
    )
```

profile of v0, /device:TPU:1, one launch (start us, length us, event | category | flops | bytes accessed | tf_op | source)
XLA Modules:
  0.0 749.0 jit_solution(9731902227004302876)
XLA Ops:
  8.0 44.9 %all_gather.6 = bf16[80,2048]{1,0:T(8,128)(2,1)S(1)} all-gather(bf16[80,128]{1,0:T(8,128)(2,1)S(1)} %pad_maximum_fusion.1), channel_id=1, replica_groups=mesh['blk'=32,'grp'=16] {'grp'}, dimensions={1}, use_global_device_ids=true | all-gather | bytes 348160 | tf_op jit(solution)/shard_map/all_gather | solution.py:78
  53.0 14.0 %collective-permute-start.2 = (bf16[80,2048]{1,0:T(8,128)(2,1)S(1)}, bf16[80,2048]{1,0:T(8,128)(2,1)S(1)}, u32[]{:S(2)}, u32[]{:S(2)}) collective-permute-start(bf16[80,2048]{1,0:T(8,128)(2,1)S(1)} %all_gather.6), channel_id=1, source_target_pairs={{48,0},{64,16},{80,32},{96,48},{112,64},{128,80},{144,96},{160,112... | collective-permute-start | bytes 983048 | tf_op jit(solution)/shard_map/ppermute | solution.py:12
  67.0 1.9 collective-permute-start.1
  68.9 2.3 collective-permute-start
  74.5 4.2 collective-permute-done
  78.7 18.1 %conditional.6 = (f32[64,128]{1,0:T(8,128)}, f32[64,2048]{1,0:T(8,128)}) conditional(s32[]{:T(128)} %bitcast, () %tuple.145, (bf16[80,2048]{1,0:T(8,128)(2,1)S(1)}, f32[16]{0:T(128)S(1)}, f32[16,128]{1,0:T(8,128)S(1)}, bf16[64,128]{1,0:T(8,128)(2,1)S(1)}) %tuple.308), branch_computations={%region_6.7_spmd, %region_7.12_spmd} | conditional | flops 30248328 | bytes 2004397 | solution.py:85
  79.7 17.1 %while.110 = (s32[]{:T(128)}, f32[64,128]{1,0:T(8,128)}, f32[64,2048]{1,0:T(8,128)}, s32[4]{0:T(128)S(1)}, bf16[64,2048]{1,0:T(8,128)(2,1)S(1)}, /*index=5*/f32[...) while((s32[]{:T(128)}, f32[64,128]{1,0:T(8,128)}, ...), condition=%wide.region_11.11_spmd.clone, body=%wide.region_9.0_spmd.clone.sunk | while | flops 30178824 | bytes 750297 | solution.py:54
  85.5 1.5 convolution_add_fusion.23
  89.9 1.5 convolution_add_fusion.23
  94.4 1.5 convolution_add_fusion.23
  96.8 1.9 collective-permute-start.3
  98.7 1.4 conditional.7
  100.1 23.3 %collective-permute-start.4 = (f32[64,2048]{1,0:T(8,128)}, f32[64,2048]{1,0:T(8,128)S(1)}, u32[]{:S(2)}, u32[]{:S(2)}) collective-permute-start(f32[64,2048]{1,0:T(8,128)} %get-tuple-element.845), channel_id=1, source_target_pairs={{480,0},{496,16},{0,32},{16,48},{32,64},{48,80},{64,96},{80,112},{... | collective-permute-start | bytes 1572872 | tf_op jit(solution)/shard_map/ppermute | solution.py:12
  123.5 18.2 %conditional.8 = (f32[64,128]{1,0:T(8,128)}, f32[64,2048]{1,0:T(8,128)}) conditional(s32[]{:T(128)} %bitcast.2, () %tuple.149, (bf16[80,2048]{1,0:T(8,128)(2,1)S(1)}, f32[16]{0:T(128)S(1)}, f32[16,128]{1,0:T(8,128)S(1)}, bf16[64,128]{1,0:T(8,128)(2,1)S(1)}) %tuple.310), branch_computations={%region_18.19_spmd, %region_19.24_spmd} | conditional | flops 30248328 | bytes 2004397 | solution.py:85
  124.5 17.1 %while.112 = (s32[]{:T(128)}, f32[64,128]{1,0:T(8,128)}, f32[64,2048]{1,0:T(8,128)}, s32[4]{0:T(128)S(1)}, bf16[64,2048]{1,0:T(8,128)(2,1)S(1)}, /*index=5*/f32[...) while((s32[]{:T(128)}, f32[64,128]{1,0:T(8,128)}, ...), condition=%wide.region_23.23_spmd.clone, body=%wide.region_21.0_spmd.clone.sunk | while | flops 30178824 | bytes 750297 | solution.py:54
  130.3 1.5 convolution_add_fusion.21
  134.8 1.5 convolution_add_fusion.21
  139.3 1.5 convolution_add_fusion.21
  141.7 3.9 collective-permute-start.5
  145.7 13.1 %collective-permute-done.5 = f32[64,2048]{1,0:T(8,128)S(1)} collective-permute-done((f32[64,2048]{1,0:T(8,128)}, f32[64,2048]{1,0:T(8,128)S(1)}, u32[]{:S(2)}, u32[]{:S(2)}) %collective-permute-start.5) | collective-permute-done | bytes 524320 | tf_op jit(solution)/shard_map/ppermute | solution.py:12
  159.7 8.8 %while.116 = (s32[]{:T(128)}, f32[64,128]{1,0:T(8,128)S(1)}, s32[4]{0:T(128)S(1)}, bf16[64,2048]{1,0:T(8,128)(2,1)S(1)}, f32[128]{0:T(128)S(1)}, /*index=5*/f32[...) while((s32[]{:T(128)}, f32[64,128]{1,0:T(8,128)S(1)}, ...), condition=%wide.region_5.6_spmd.clone, body=%wide.region_3.5_spmd.clone.sunk | while | flops 21790216 | bytes 471749 | solution.py:54
  168.6 68.9 %reduce-scatter.3.cloned.1.call-done = f32[64,128]{1,0:T(8,128)} async-done(((f32[64,2048]{1,0:T(8,128)}), f32[64,128]{1,0:T(8,128)}) %reduce-scatter.3.cloned.1.call-update) | async-done | bytes 32784 | tf_op jit(solution)/shard_map/reduce_scatter | solution.py:95
  239.1 97.5 %all-reduce = (f32[64]{0:T(128)S(1)}, f32[64]{0:T(128)S(1)}) all-reduce(f32[64]{0:T(128)S(1)} %get-tuple-element.1083, f32[64]{0:T(128)S(1)} %get-tuple-element.1082), channel_id=1, replica_groups=mesh['blk'=32,'grp'=16] {'blk','grp'}, use_global_device_ids=true, to_apply=%region_1.0 | all-reduce | flops 128 | bytes 1024 | tf_op jit(solution)/shard_map/psum | solution.py:69
  336.7 94.2 %psum.30 = f32[64]{0:T(128)S(1)} all-reduce(f32[64]{0:T(128)S(1)} %multiply_reduce_fusion.15), channel_id=1, replica_groups=mesh['blk'=32,'grp'=16] {'blk','grp'}, use_global_device_ids=true, to_apply=%region_28.29 | all-reduce | flops 64 | bytes 512 | tf_op jit(solution)/shard_map/psum | solution.py:69
  431.0 36.4 %all_gather.7 = bf16[80,2048]{1,0:T(8,128)(2,1)S(1)} all-gather(bf16[80,128]{1,0:T(8,128)(2,1)S(1)} %pad_maximum_fusion), channel_id=1, replica_groups=mesh['blk'=32,'grp'=16] {'grp'}, dimensions={1}, use_global_device_ids=true | all-gather | bytes 348160 | tf_op jit(solution)/shard_map/all_gather | solution.py:78
  467.4 9.2 %collective-permute-start.6 = (bf16[80,2048]{1,0:T(8,128)(2,1)S(1)}, bf16[80,2048]{1,0:T(8,128)(2,1)S(1)}, u32[]{:S(2)}, u32[]{:S(2)}) collective-permute-start(bf16[80,2048]{1,0:T(8,128)(2,1)S(1)} %all_gather.7), channel_id=1, source_target_pairs={{16,0},{32,16},{48,32},{64,48},{80,64},{96,80},{112,96},{128,112},... | collective-permute-start | bytes 983048 | tf_op jit(solution)/shard_map/ppermute | solution.py:12
  476.7 3.1 collective-permute-start.7
  479.8 3.7 collective-permute-start.8
  483.5 1.1 collective-permute-done.6
  484.6 18.1 %conditional.9 = (f32[64,128]{1,0:T(8,128)}, f32[64,2048]{1,0:T(8,128)}) conditional(s32[]{:T(128)} %bitcast, () %tuple.152, (bf16[80,2048]{1,0:T(8,128)(2,1)S(1)}, f32[16]{0:T(128)S(1)}, f32[16,128]{1,0:T(8,128)S(1)}, bf16[64,128]{1,0:T(8,128)(2,1)S(1)}) %tuple.311), branch_computations={%region_32.33_spmd, %region_33.38_spmd} | conditional | flops 30248328 | bytes 2004397 | solution.py:85
  485.6 17.1 %while.113 = (s32[]{:T(128)}, f32[64,128]{1,0:T(8,128)}, f32[64,2048]{1,0:T(8,128)}, s32[4]{0:T(128)S(1)}, bf16[64,2048]{1,0:T(8,128)(2,1)S(1)}, /*index=5*/f32[...) while((s32[]{:T(128)}, f32[64,128]{1,0:T(8,128)}, ...), condition=%wide.region_37.37_spmd.clone, body=%wide.region_35.36_spmd.clone.sunk | while | flops 30178824 | bytes 750297 | solution.py:54
  491.4 1.5 convolution_add_fusion.20
  495.9 1.5 convolution_add_fusion.20
  500.3 1.5 convolution_add_fusion.20
  502.7 1.9 collective-permute-start.9
  504.6 1.4 conditional.10
  506.1 18.6 %collective-permute-start.10 = (f32[64,2048]{1,0:T(8,128)}, f32[64,2048]{1,0:T(8,128)S(1)}, u32[]{:S(2)}, u32[]{:S(2)}) collective-permute-start(f32[64,2048]{1,0:T(8,128)} %get-tuple-element.852), channel_id=1, source_target_pairs={{480,0},{496,16},{0,32},{16,48},{32,64},{48,80},{64,96},{80,112},{... | collective-permute-start | bytes 1572872 | tf_op jit(solution)/shard_map/ppermute | solution.py:12
  524.6 17.9 %conditional.11 = (f32[64,128]{1,0:T(8,128)}, f32[64,2048]{1,0:T(8,128)}) conditional(s32[]{:T(128)} %bitcast.2, () %tuple.156, (bf16[80,2048]{1,0:T(8,128)(2,1)S(1)}, f32[16]{0:T(128)S(1)}, f32[16,128]{1,0:T(8,128)S(1)}, bf16[64,128]{1,0:T(8,128)(2,1)S(1)}) %tuple.313), branch_computations={%region_44.45_spmd, %region_45.50_spmd} | conditional | flops 30248328 | bytes 2004397 | solution.py:85
  525.7 16.8 %while.115 = (s32[]{:T(128)}, f32[64,128]{1,0:T(8,128)}, f32[64,2048]{1,0:T(8,128)}, s32[4]{0:T(128)S(1)}, bf16[64,2048]{1,0:T(8,128)(2,1)S(1)}, /*index=5*/f32[...) while((s32[]{:T(128)}, f32[64,128]{1,0:T(8,128)}, ...), condition=%wide.region_49.49_spmd.clone, body=%wide.region_47.48_spmd.clone.sunk | while | flops 30178824 | bytes 750297 | solution.py:54
  531.3 1.5 convolution_add_fusion.18
  535.7 1.5 convolution_add_fusion.18
  540.1 1.5 convolution_add_fusion.18
  542.5 4.3 collective-permute-start.11
  546.9 12.7 %collective-permute-done.11 = f32[64,2048]{1,0:T(8,128)S(1)} collective-permute-done((f32[64,2048]{1,0:T(8,128)}, f32[64,2048]{1,0:T(8,128)S(1)}, u32[]{:S(2)}, u32[]{:S(2)}) %collective-permute-start.11) | collective-permute-done | bytes 524320 | tf_op jit(solution)/shard_map/ppermute | solution.py:12
  560.6 8.8 %while.117 = (s32[]{:T(128)}, f32[64,128]{1,0:T(8,128)S(1)}, s32[4]{0:T(128)S(1)}, bf16[64,2048]{1,0:T(8,128)(2,1)S(1)}, f32[128]{0:T(128)S(1)}, /*index=5*/f32[...) while((s32[]{:T(128)}, f32[64,128]{1,0:T(8,128)S(1)}, ...), condition=%wide.region_31.32_spmd.clone, body=%wide.region_29.31_spmd.clone.sunk | while | flops 21790216 | bytes 471749 | solution.py:54
  569.4 73.6 %reduce-scatter.5.cloned.1.call-done = f32[64,128]{1,0:T(8,128)} async-done(((f32[64,2048]{1,0:T(8,128)}), f32[64,128]{1,0:T(8,128)}) %reduce-scatter.5.cloned.1.call-update) | async-done | bytes 32784 | tf_op jit(solution)/shard_map/reduce_scatter | solution.py:95
  643.0 0.9 multiply_reduce_fusion.14
  643.9 97.5 %psum.31 = f32[64]{0:T(128)S(1)} all-reduce(f32[64]{0:T(128)S(1)} %get-tuple-element.1222), channel_id=1, replica_groups=mesh['blk'=32,'grp'=16] {'blk','grp'}, use_global_device_ids=true, to_apply=%region_52.53 | all-reduce | flops 64 | bytes 512 | tf_op jit(solution)/shard_map/psum | solution.py:97
  (174 shorter events, 64.2 us)
Async XLA Ops:
  7.2 0.8 copy-start.2
  7.2 230.3 %reduce-scatter.3.cloned.1.call-start = ((), (), s32[]{:S(2)}) async-start(), calls=%async_computation.2 | async-start | bytes 557056 | tf_op jit(solution)/shard_map/reduce_scatter | solution.py:95
  8.0 63.3 %copy-start.4 = (s32[32,3]{0,1:T(4,128)S(1)}, s32[32,3]{0,1:T(4,128)}, u32[]{:S(2)}) copy-start(s32[32,3]{0,1:T(4,128)} %param.37) | copy-start | bytes 1156
  53.0 70.5 %collective-permute-start.2 = (bf16[80,2048]{1,0:T(8,128)(2,1)S(1)}, bf16[80,2048]{1,0:T(8,128)(2,1)S(1)}, u32[]{:S(2)}, u32[]{:S(2)}) collective-permute-start(bf16[80,2048]{1,0:T(8,128)(2,1)S(1)} %all_gather.6), channel_id=1, source_target_pairs={{48,0},{64,16},{80,32},{96,48},{112,64},{128,80},{144,96},{160,112... | collective-permute-start | bytes 983048 | tf_op jit(solution)/shard_map/ppermute | solution.py:12
  67.0 31.7 %collective-permute-start.1 = (bf16[80,2048]{1,0:T(8,128)(2,1)S(1)}, bf16[80,2048]{1,0:T(8,128)(2,1)S(1)}, u32[]{:S(2)}, u32[]{:S(2)}) collective-permute-start(bf16[80,2048]{1,0:T(8,128)(2,1)S(1)} %all_gather.6), channel_id=1, source_target_pairs={{32,0},{48,16},{64,32},{80,48},{96,64},{112,80},{128,96},{144,112}... | collective-permute-start | bytes 983048 | tf_op jit(solution)/shard_map/ppermute | solution.py:12
  68.9 9.8 %collective-permute-start = (bf16[80,2048]{1,0:T(8,128)(2,1)S(1)}, bf16[80,2048]{1,0:T(8,128)(2,1)S(1)}, u32[]{:S(2)}, u32[]{:S(2)}) collective-permute-start(bf16[80,2048]{1,0:T(8,128)(2,1)S(1)} %all_gather.6), channel_id=1, source_target_pairs={{16,0},{32,16},{48,32},{64,48},{80,64},{96,80},{112,96},{128,112},... | collective-permute-start | bytes 983048 | tf_op jit(solution)/shard_map/ppermute | solution.py:12
  73.8 0.7 copy-start.1
  96.8 48.9 %collective-permute-start.3 = (f32[64,2048]{1,0:T(8,128)}, f32[64,2048]{1,0:T(8,128)S(1)}, u32[]{:S(2)}, u32[]{:S(2)}) collective-permute-start(f32[64,2048]{1,0:T(8,128)} %get-tuple-element.844), channel_id=1, source_target_pairs={{496,0},{0,16},{16,32},{32,48},{48,64},{64,80},{80,96},{96,112},{1... | collective-permute-start | bytes 1572872 | tf_op jit(solution)/shard_map/ppermute | solution.py:12
  100.1 45.5 %collective-permute-start.4 = (f32[64,2048]{1,0:T(8,128)}, f32[64,2048]{1,0:T(8,128)S(1)}, u32[]{:S(2)}, u32[]{:S(2)}) collective-permute-start(f32[64,2048]{1,0:T(8,128)} %get-tuple-element.845), channel_id=1, source_target_pairs={{480,0},{496,16},{0,32},{16,48},{32,64},{48,80},{64,96},{80,112},{... | collective-permute-start | bytes 1572872 | tf_op jit(solution)/shard_map/ppermute | solution.py:12
  141.7 17.1 %collective-permute-start.5 = (f32[64,2048]{1,0:T(8,128)}, f32[64,2048]{1,0:T(8,128)S(1)}, u32[]{:S(2)}, u32[]{:S(2)}) collective-permute-start(f32[64,2048]{1,0:T(8,128)} %get-tuple-element.846), channel_id=1, source_target_pairs={{464,0},{480,16},{496,32},{0,48},{16,64},{32,80},{48,96},{64,112},... | collective-permute-start | bytes 1572872 | tf_op jit(solution)/shard_map/ppermute | solution.py:12
  159.6 483.4 %reduce-scatter.5.cloned.1.call-start = ((), (), s32[]{:S(2)}) async-start(), calls=%async_computation.3 | async-start | bytes 557056 | tf_op jit(solution)/shard_map/reduce_scatter | solution.py:95
  159.7 77.8 %copy-start = (f32[64,128]{1,0:T(8,128)S(1)}, f32[64,128]{1,0:T(8,128)}, u32[]{:S(2)}) copy-start(f32[64,128]{1,0:T(8,128)} %param.34) | copy-start | bytes 98308
  237.5 0.7 copy-start.3
  467.4 17.2 %collective-permute-start.6 = (bf16[80,2048]{1,0:T(8,128)(2,1)S(1)}, bf16[80,2048]{1,0:T(8,128)(2,1)S(1)}, u32[]{:S(2)}, u32[]{:S(2)}) collective-permute-start(bf16[80,2048]{1,0:T(8,128)(2,1)S(1)} %all_gather.7), channel_id=1, source_target_pairs={{16,0},{32,16},{48,32},{64,48},{80,64},{96,80},{112,96},{128,112},... | collective-permute-start | bytes 983048 | tf_op jit(solution)/shard_map/ppermute | solution.py:12
  476.7 27.9 %collective-permute-start.7 = (bf16[80,2048]{1,0:T(8,128)(2,1)S(1)}, bf16[80,2048]{1,0:T(8,128)(2,1)S(1)}, u32[]{:S(2)}, u32[]{:S(2)}) collective-permute-start(bf16[80,2048]{1,0:T(8,128)(2,1)S(1)} %all_gather.7), channel_id=1, source_target_pairs={{32,0},{48,16},{64,32},{80,48},{96,64},{112,80},{128,96},{144,112}... | collective-permute-start | bytes 983048 | tf_op jit(solution)/shard_map/ppermute | solution.py:12
  479.8 44.8 %collective-permute-start.8 = (bf16[80,2048]{1,0:T(8,128)(2,1)S(1)}, bf16[80,2048]{1,0:T(8,128)(2,1)S(1)}, u32[]{:S(2)}, u32[]{:S(2)}) collective-permute-start(bf16[80,2048]{1,0:T(8,128)(2,1)S(1)} %all_gather.7), channel_id=1, source_target_pairs={{48,0},{64,16},{80,32},{96,48},{112,64},{128,80},{144,96},{160,112... | collective-permute-start | bytes 983048 | tf_op jit(solution)/shard_map/ppermute | solution.py:12
  502.7 44.2 %collective-permute-start.9 = (f32[64,2048]{1,0:T(8,128)}, f32[64,2048]{1,0:T(8,128)S(1)}, u32[]{:S(2)}, u32[]{:S(2)}) collective-permute-start(f32[64,2048]{1,0:T(8,128)} %get-tuple-element.851), channel_id=1, source_target_pairs={{496,0},{0,16},{16,32},{32,48},{48,64},{64,80},{80,96},{96,112},{1... | collective-permute-start | bytes 1572872 | tf_op jit(solution)/shard_map/ppermute | solution.py:12
  506.1 40.9 %collective-permute-start.10 = (f32[64,2048]{1,0:T(8,128)}, f32[64,2048]{1,0:T(8,128)S(1)}, u32[]{:S(2)}, u32[]{:S(2)}) collective-permute-start(f32[64,2048]{1,0:T(8,128)} %get-tuple-element.852), channel_id=1, source_target_pairs={{480,0},{496,16},{0,32},{16,48},{32,64},{48,80},{64,96},{80,112},{... | collective-permute-start | bytes 1572872 | tf_op jit(solution)/shard_map/ppermute | solution.py:12
  542.5 17.2 %collective-permute-start.11 = (f32[64,2048]{1,0:T(8,128)}, f32[64,2048]{1,0:T(8,128)S(1)}, u32[]{:S(2)}, u32[]{:S(2)}) collective-permute-start(f32[64,2048]{1,0:T(8,128)} %get-tuple-element.853), channel_id=1, source_target_pairs={{464,0},{480,16},{496,32},{0,48},{16,64},{32,80},{48,96},{64,112},... | collective-permute-start | bytes 1572872 | tf_op jit(solution)/shard_map/ppermute | solution.py:12
Sparse Core Ops, SparseCore 0:
  159.8 77.6 reduce-scatter.2
  560.7 82.2 reduce-scatter.4
where the time goes:
time: 751 us; the launch traced here: 749 us
  blocking collectives  370 us (49%)
  waiting for transfers between devices  174 us (23%)
  starting transfers between devices  88.2 us (12%)
  matrix products  52.8 us (7%)
  local copies, waits for them, and re-layouts  22.9 us (3%)
  loops' own time  16.7 us (2%)
  between operations  16.3 us (2%)
  other arithmetic  7.84 us (1%)
    psum x2, blocking collectives, squares(): return lax.psum(jnp.sum(values * values, axis=1), ('blk', 'grp'))  192 us
    reduce_scatter x2, waiting for transfers between devices, on_device(): lax.psum_scatter(incoming, 'grp', scatter_dimension=1, tiled=True)  142 us
    psum x1, blocking collectives, on_device(): lax.psum(jnp.sum(direction * image, axis=1), ('blk', 'grp'))  97.5 us
    ppermute x12, starting transfers between devices, passed_along(): return lax.ppermute(block, axis, route)  88.2 us
    all_gather x2, blocking collectives, on_device(): own = lax.all_gather(stacked, 'grp', axis=1, tiled=True)  81.3 us
    ppermute x12, waiting for transfers between devices, passed_along(): return lax.ppermute(block, axis, route)  31.1 us
    dot_general x24, matrix products, step(): lax.dot_general(part_v, tile, (((1,), (1,)), ((), ())), preferred_element...  23 us
    another operation x6, loops' own time, tile_terms(): lax.scan(step, start_carry, jnp.arange(count, dtype=jnp.int32))  16.6 us
  transfers between devices with their start and end apart: 14, of which 6 were waited for; matrix products, arithmetic and copies ran while one was open for 10% of the time, Pallas kernels for 0%

commit v1 on v0

v1 whole, which is shorter than its diff:
```python
import jax
import jax.numpy as jnp
from jax import lax
from jax.experimental import pallas as pl
from jax.experimental.pallas import tpu as pltpu
from jax.sharding import PartitionSpec as P

MESH = pl.DeviceIdType.MESH
F32 = jnp.float32
BF16 = jnp.bfloat16
STEP = 0.38
FAR = 64.0
PIECE = 128
NRHS = 64
FEAT = 16
AMP = 1.0 / 2064.0 / 256.0


def split3(value):
    first = value.astype(BF16).astype(F32)
    rest = value - first
    second = rest.astype(BF16).astype(F32)
    return first, second, rest - second


def kernel(
    points_ref, right_ref, nugget_ref, scales_ref, pairs_ref,
    x_ref, res_ref,
    col_pts, row_pts, right_v, nugget_v, scales_s, pairs_s, pen_s,
    inv_v, row_ops, col_ops, tiles,
    v1, v2, p_rows, out1, out2, sib1, sib2, got1, got2, sib_got1, sib_got2, ar,
    local_sem, pts_send, pts_recv, rpts_send, rpts_recv, v1_send, v1_recv, v2_send, v2_recv,
    pr_send, pr_recv, sib_send, sib_recv, rs_send, rs_recv, ar_send, ar_recv,
):
    blk, grp = lax.axis_index("blk"), lax.axis_index("grp")
    chip, core = blk // 2, blk % 2
    side = 1 - 2 * core
    zlow = chip % 2
    zhigh, xat = grp // 4, grp % 4

    def device(chip_at, core_at, zhigh_at, x_at):
        return (
            lax.rem(chip_at + 32, 16) * 2 + core_at,
            lax.rem(zhigh_at + 8, 4) * 4 + lax.rem(x_at + 8, 4),
        )

    col_to = [
        device(chip + dm, cc, zhigh, xat + dx)
        for dm, cc in ((0, core), (side, core), (-side, 1 - core), (-2 * side, 1 - core))
        for dx in range(4)
    ]
    col_from = [
        device(chip - dm, cc, zhigh, xat - dx)
        for dm, cc in ((0, core), (side, core), (side, 1 - core), (2 * side, 1 - core))
        for dx in range(4)
    ]
    row_to = [device(chip, cc, zhigh + k, xat) for cc in (core, 1 - core) for k in range(4)]
    sum_to = [device(chip, core, zhigh - k, xat) for k in range(4)]
    sibling = device(chip, 1 - core, zhigh, xat)
    y_line = [device(chip + 2 * k, core, zhigh, xat) for k in range(8)]
    z_line = [
        device(chip + dz * (1 - 2 * zlow), core, zhigh + k, xat) for dz in range(2) for k in range(4)
    ]
    x_line = [device(chip, cc, zhigh, xat + k) for cc in (core, 1 - core) for k in range(4)]

    greet = col_from[1:] + y_line[1:] + z_line[1:] + x_line[4:] + row_to[5:]
    barrier = pltpu.get_barrier_semaphore()
    for target in greet:
        pl.semaphore_signal(barrier, inc=1, device_id=target, device_id_type=MESH)

    loads = [
        pltpu.make_async_copy(points_ref, col_pts.at[0], local_sem.at[0]),
        pltpu.make_async_copy(right_ref, right_v, local_sem.at[1]),
        pltpu.make_async_copy(scales_ref, scales_s, local_sem.at[2]),
        pltpu.make_async_copy(pairs_ref, pairs_s, local_sem.at[3]),
        pltpu.make_async_copy(nugget_ref, nugget_v, local_sem.at[4]),
    ]
    for load in loads:
        load.start()

    def remote(src, dst, send, recv, target):
        return pltpu.make_async_remote_copy(
            src_ref=src, dst_ref=dst, send_sem=send, recv_sem=recv, device_id=target, device_id_type=MESH
        )

    def lanes(ref, index):
        return ref.at[:, pl.ds(index * PIECE, PIECE)]

    loads[0].wait()
    pl.semaphore_wait(barrier, len(greet))
    row_copies = [
        remote(col_pts.at[0], row_pts.at[k], rpts_send.at[k], rpts_recv.at[k], row_to[k]) for k in range(1, 8)
    ]
    col_copies = [
        remote(col_pts.at[0], col_pts.at[i], pts_send.at[i], pts_recv.at[i], col_to[i]) for i in range(1, 16)
    ]
    for copy in row_copies + col_copies:
        copy.start()
    row_pts[0] = col_pts[0]

    loads[1].wait()
    v1[:, 0:PIECE] = right_v[...].astype(BF16)
    v1_copies = [
        remote(lanes(v1, 0), lanes(v1, i), v1_send.at[i], v1_recv.at[i], col_to[i]) for i in range(1, 16)
    ]
    for copy in v1_copies:
        copy.start()

    for load in loads[2:]:
        load.wait()
    for f in range(FEAT):
        inv_v[f : f + 1, :] = jnp.full((1, PIECE), scales_s[f], F32)
    inv_v[...] = 1.0 / (inv_v[...] * inv_v[...])

    def away(low, offset):
        value = pairs_s[lax.rem(low + 32, 32), offset - 1]
        return (1 - value).astype(F32) * FAR

    first = core == 0
    pen_s[0] = 0.0
    pen_s[1] = away(jnp.where(first, blk - 2, blk), 2)
    pen_s[2] = away(jnp.where(first, blk - 1, blk), 1)
    pen_s[3] = away(jnp.where(first, blk - 3, blk), 3)
    pen_s[4] = away(jnp.where(first, blk, blk - 1), 1)
    pen_s[5] = away(jnp.where(first, blk - 2, blk - 1), 3)
    pen_s[6] = away(jnp.where(first, blk - 1, blk - 1), 2)
    pen_s[7] = FAR

    at_row = lax.broadcasted_iota(jnp.int32, (FEAT, PIECE), 0)

    def norm_rows(pts):
        norm = jnp.sum(pts * pts * (16.0 * inv_v[...]), axis=0, keepdims=True)
        return [jnp.broadcast_to(part, (FEAT, PIECE)) for part in split3(norm)]

    for k in range(8):
        if k:
            row_copies[k - 1].wait_recv()
        pts = row_pts[k].astype(F32)
        one, two, three = norm_rows(pts)
        own = at_row == (6 if k < 4 else 7)
        extra = jnp.where((at_row < 3) | own, 1.0, 0.0)
        extra = jnp.where(at_row == 3, one, extra)
        extra = jnp.where(at_row == 4, two, extra)
        extra = jnp.where(at_row == 5, three, extra)
        span = slice(k * PIECE, (k + 1) * PIECE)
        for part in range(3):
            row_ops[part * FEAT : (part + 1) * FEAT, span] = row_pts[k]
        row_ops[3 * FEAT :, span] = extra.astype(BF16)

    def column(i, chunks):
        @pl.when(i > 0)
        def _():
            remote(col_pts.at[0], col_pts.at[i], pts_send.at[i], pts_recv.at[i], sibling).wait_recv()

        pts = col_pts[i].astype(F32)
        scaled = split3(pts * (-32.0 * inv_v[...]))
        one, two, three = norm_rows(pts)
        extra = jnp.where(at_row == 0, one, 0.0)
        extra = jnp.where(at_row == 1, two, extra)
        extra = jnp.where(at_row == 2, three, extra)
        extra = jnp.where((at_row >= 3) & (at_row < 6), 1.0, extra)
        extra = jnp.where(at_row == 6, pen_s[i // 4], extra)
        extra = jnp.where(at_row == 7, pen_s[i // 4 + 4], extra)
        for part in range(3):
            col_ops[part * FEAT : (part + 1) * FEAT, :] = scaled[part].astype(BF16)
        col_ops[3 * FEAT :, :] = extra.astype(BF16)
        start = pl.multiple_of(i * PIECE, PIECE)
        ops = col_ops[...]
        for chunk in range(chunks):
            span = slice(chunk * 256, (chunk + 1) * 256)
            squared = lax.dot_general(
                ops, row_ops[:, span], (((0,), (0,)), ((), ())), preferred_element_type=F32
            )
            squared = jnp.maximum(squared, 1e-12)
            spare = jnp.maximum(4.0 - squared * lax.rsqrt(squared), 0.0)
            second = spare * spare
            tiles[pl.ds(start, PIECE), span] = (second * second * (5.0 - spare)).astype(BF16)

    def column_all(i, carry):
        column(i, 4)
        return carry

    def column_own(i, carry):
        column(i, 2)
        return carry

    lax.fori_loop(0, 12, column_all, 0)
    lax.fori_loop(12, 16, column_own, 0)

    def apply(vec, sib, sib_got, out, got, which):
        mixed = jnp.dot(vec[:, :1536], tiles[:1536, 512:], preferred_element_type=F32)
        for k in range(4):
            sib[k] = mixed[:, k * PIECE : (k + 1) * PIECE]
        swap = remote(sib, sib_got, sib_send.at[which], sib_recv.at[which], sibling)
        swap.start()
        total = jnp.dot(vec[...], tiles[:, :512], preferred_element_type=F32)
        for k in range(4):
            out[k] = total[:, k * PIECE : (k + 1) * PIECE]
        return swap

    def spread(swap, sib_got, out, got, which):
        swap.wait_recv()
        copies = []
        for k in (2, 1, 3):
            out[k] = out[k] + sib_got[k]
            copies.append(
                remote(out.at[k], got.at[k], rs_send.at[4 * which + k], rs_recv.at[4 * which + k], sum_to[k])
            )
            copies[-1].start()
        return copies

    def collect(copies, sib_got, out, got):
        mine = out[0] + sib_got[0]
        for copy in copies:
            copy.wait_recv()
        return mine + got[1] + got[2] + got[3]

    for copy in v1_copies:
        copy.wait_recv()
    swap1 = apply(v1, sib1, sib_got1, out1, got1, 0)
    sums1 = spread(swap1, sib_got1, out1, got1, 0)
    right = right_v[...]
    nugget = jnp.broadcast_to(nugget_v[...], (NRHS, PIECE))
    image = nugget * right + AMP * collect(sums1, sib_got1, out1, got1)
    step_to = right - STEP * image
    rounded = step_to.astype(BF16)
    v2[:, 0:PIECE] = rounded
    p_rows[:, 0:PIECE] = rounded
    v2_copies = [
        remote(lanes(v2, 0), lanes(v2, i), v2_send.at[i], v2_recv.at[i], col_to[i]) for i in range(1, 16)
    ]
    pr_copies = [
        remote(lanes(v2, 0), lanes(p_rows, k), pr_send.at[k], pr_recv.at[k], row_to[k]) for k in range(1, 8)
    ]
    for copy in v2_copies + pr_copies:
        copy.start()

    ones = jnp.ones((8, PIECE), F32)

    def across(values):
        return lax.dot_general(
            ones, values, (((1,), (1,)), ((), ())), precision=lax.Precision.HIGHEST, preferred_element_type=F32
        )

    sums_a = across(jnp.concatenate([right * right, right * image], axis=0))
    ar[0, 0:1, :] = sums_a[0:1]

    for copy in v2_copies:
        copy.wait_recv()
    swap2 = apply(v2, sib2, sib_got2, out2, got2, 1)
    for copy in pr_copies:
        copy.wait_recv()
    form = jnp.zeros((NRHS, PIECE), F32)
    for k in range(4):
        form = form + p_rows[:, k * PIECE : (k + 1) * PIECE].astype(F32) * out2[k]
        form = form + p_rows[:, (k + 4) * PIECE : (k + 5) * PIECE].astype(F32) * sib2[k]
    form = nugget * step_to * step_to + AMP * form
    sums_b = across(jnp.concatenate([step_to * step_to, form], axis=0))
    ar[0, 1:2, :] = sums_b[0:1]

    def share(stage, line):
        copies = [
            remote(
                ar.at[8 * stage], ar.at[8 * stage + k],
                ar_send.at[8 * stage + k], ar_recv.at[8 * stage + k], line[k],
            )
            for k in range(1, 8)
        ]
        for copy in copies:
            copy.start()
        return copies

    def gathered(stage, copies):
        for copy in copies:
            copy.wait_recv()
        total = ar[8 * stage]
        for k in range(1, 8):
            total = total + ar[8 * stage + k]
        return total

    shares_y = share(0, y_line)
    sums2 = spread(swap2, sib_got2, out2, got2, 1)
    ar[8] = gathered(0, shares_y)
    shares_x = share(1, x_line)
    ar[16] = gathered(1, shares_x)
    shares_z = share(2, z_line)
    second_image = nugget * step_to + AMP * collect(sums2, sib_got2, out2, got2)
    total = gathered(2, shares_z)

    top, low = total[0:1], total[1:2]
    rr, ru = top, pltpu.roll(top, 64, 1)
    pp, pw = low, pltpu.roll(low, 64, 1)
    alpha = rr / ru
    share_p = alpha / STEP
    share_r = 1.0 - share_p
    rp = rr - STEP * ru
    pu = (rp - pp) / STEP
    rr_next = share_r * share_r * rr + 2.0 * share_r * share_p * rp + share_p * share_p * pp
    dir_r = share_r + rr_next / rr
    bend = dir_r * dir_r * ru + 2.0 * dir_r * share_p * pu + share_p * share_p * pw
    alpha_next = rr_next / bend
    along = alpha_next * dir_r
    coefs = jnp.concatenate(
        [
            alpha + along,
            alpha_next * share_p,
            share_r - along / STEP,
            share_p + along / STEP,
            -alpha_next * share_p,
            jnp.zeros((3, PIECE), F32),
        ],
        axis=0,
    )
    columns = coefs.T[:NRHS]
    x_ref[...] = columns[:, 0:1] * right + columns[:, 1:2] * step_to
    res_ref[...] = columns[:, 2:3] * right + columns[:, 3:4] * step_to + columns[:, 4:5] * second_image

    for copy in (
        row_copies + col_copies + v1_copies + sums1 + v2_copies + pr_copies + sums2
        + [swap1, swap2] + shares_y + shares_x + shares_z
    ):
        copy.wait_send()


def on_device(points, right_side, nugget, scales, pairs):
    dma = pltpu.SemaphoreType.DMA
    any_space = pl.BlockSpec(memory_space=pl.ANY)
    vmem = pl.BlockSpec(memory_space=pltpu.VMEM)
    return pl.pallas_call(
        kernel,
        out_shape=(
            jax.ShapeDtypeStruct((NRHS, PIECE), F32),
            jax.ShapeDtypeStruct((NRHS, PIECE), F32),
        ),
        in_specs=[any_space] * 5,
        out_specs=(vmem, vmem),
        scratch_shapes=[
            pltpu.VMEM((16, FEAT, PIECE), BF16),
            pltpu.VMEM((8, FEAT, PIECE), BF16),
            pltpu.VMEM((NRHS, PIECE), F32),
            pltpu.VMEM((1, PIECE), F32),
            pltpu.SMEM((FEAT,), F32),
            pltpu.SMEM((32, 3), jnp.int32),
            pltpu.SMEM((8,), F32),
            pltpu.VMEM((FEAT, PIECE), F32),
            pltpu.VMEM((4 * FEAT, 8 * PIECE), BF16),
            pltpu.VMEM((4 * FEAT, PIECE), BF16),
            pltpu.VMEM((16 * PIECE, 8 * PIECE), BF16),
            pltpu.VMEM((NRHS, 16 * PIECE), BF16),
            pltpu.VMEM((NRHS, 16 * PIECE), BF16),
            pltpu.VMEM((NRHS, 8 * PIECE), BF16),
        ]
        + [pltpu.VMEM((4, NRHS, PIECE), F32)] * 8
        + [
            pltpu.VMEM((24, 2, PIECE), F32),
            dma((5,)),
            dma((16,)), dma((16,)), dma((8,)), dma((8,)),
            dma((16,)), dma((16,)), dma((16,)), dma((16,)),
            dma((8,)), dma((8,)),
            dma((2,)), dma((2,)), dma((8,)), dma((8,)), dma((24,)), dma((24,)),
        ],
        compiler_params=pltpu.CompilerParams(
            collective_id=0, has_side_effects=True, vmem_limit_bytes=40 * 2**20
        ),
    )(points, right_side, nugget.reshape(1, PIECE), scales, pairs)


def solution(mesh):
    placed = (P(None, ("blk", "grp")), P(None, ("blk", "grp")), P(("blk", "grp")), P(), P())
    return jax.shard_map(
        on_device,
        mesh=mesh,
        in_specs=placed,
        out_specs=(P(None, ("blk", "grp")), P(None, ("blk", "grp"))),
        check_vma=False,
    )
```

time: 751 us -> 62 us (0.08)
  blocking collectives: 370 us -> 0 us
  waiting for transfers between devices: 174 us -> 0 us
  starting transfers between devices: 88.2 us -> 0 us
  Pallas kernels: 0 us -> 58.3 us
  matrix products: 52.8 us -> 0 us
  local copies, waits for them, and re-layouts: 22.9 us -> 2.78 us
  loops' own time: 16.7 us -> 0 us
  between operations: 16.3 us -> 0.68 us
  other arithmetic: 7.84 us -> 0 us
    psum x3 -> x0, blocking collectives: 289 us -> none  [the longest x2 192 us: squares(): return lax.psum(jnp.sum(values * values, axis=1), ('blk', 'grp'))]
    reduce_scatter x2 -> x0, waiting for transfers between devices: 142 us -> none  [on_device(): lax.psum_scatter(incoming, 'grp', scatter_dimension=1, tiled=True)]
    ppermute x12 -> x0, starting transfers between devices: 88.2 us -> none  [passed_along(): return lax.ppermute(block, axis, route)]
    all_gather x2 -> x0, blocking collectives: 81.3 us -> none  [on_device(): own = lax.all_gather(stacked, 'grp', axis=1, tiled=True)]
    pallas_call x0 -> x1, Pallas kernels: none -> 58.3 us  [on_device(): pl.pallas_call(kernel, out_shape=(jax.ShapeDtypeStruct((NRHS, PIECE), F32...]
    dot_general x64 -> x0, matrix products: 52.8 us -> none  [the longest x24 23 us: step(): lax.dot_general(part_v, tile, (((1,), (1,)), ((), ())), preferred_element...]
    ppermute x12 -> x0, waiting for transfers between devices: 31.1 us -> none  [passed_along(): return lax.ppermute(block, axis, route)]
    another operation x12 -> x0, loops' own time: 16.7 us -> none  [the longest x6 16.6 us: tile_terms(): lax.scan(step, start_carry, jnp.arange(count, dtype=jnp.int32))]
  transfers between devices with their start and end apart: 14 -> 0, of which waited for: 6 -> 0; matrix products, arithmetic and copies ran while one was open for 10% -> 0% of each run, Pallas kernels for 0% -> 0%
where the time goes in v1:
time: 62 us; the launch traced here: 61.7 us
  Pallas kernels  58.3 us (94%)
  local copies, waits for them, and re-layouts  2.78 us (4%)
  between operations  0.68 us (1%)
    pallas_call x1, Pallas kernels, on_device(): pl.pallas_call(kernel, out_shape=(jax.ShapeDtypeStruct((NRHS, PIECE), F32...  58.3 us
    unnamed x11, local copies, waits for them, and re-layouts  2.78 us

profile of v1, /device:TPU:1, one launch (start us, length us, event | category | flops | bytes accessed | tf_op | source)
XLA Modules:
  0.0 61.7 jit_solution(10310437605016894692)
XLA Ops:
  0.6 0.0 copy-start.1
  0.6 0.0 copy-start.2
  0.7 0.0 copy-start.3
  0.7 0.8 %copy.7.pairs_ref = s32[32,3]{1,0:T(8,128)S(1)} copy(s32[32,3]{0,1:T(4,128)} %param.9) | data formatting | bytes 768 | tf_op args[4]
  1.4 0.0 copy-done.1
  1.4 0.0 copy-done.2
  1.4 0.0 copy-done.3
  1.5 0.0 copy-start
  1.5 0.7 %copy-done = f32[64,128]{1,0:T(8,128)S(1)} copy-done((f32[64,128]{1,0:T(8,128)S(1)}, f32[64,128]{1,0:T(8,128)}, u32[]{:S(2)}) %copy-start) | copy-done | bytes 32792
  2.2 58.3 %shard_map.68 = (f32[64,128]{1,0:T(8,128)S(1)}, f32[64,128]{1,0:T(8,128)S(1)}) custom-call(bf16[16,128]{1,0:T(8,128)(2,1)S(1)} %copy-done.1, f32[64,128]{1,0:T(8,128)S(1)} %copy-done, f32[1,128]{1,0:T(1,128)S(1)} %bitcast.1, f32[16]{0:T(128)S(1)} %copy-done.3, s32[32,3]{1,0:T(8,128)S(1)} %copy.7.pairs_ref), custom_call_target="tpu_custom_call" | custom-call | tf_op jit(solution)/shard_map/pallas_call | solution.py:329
  60.5 0.6 copy.10
  61.1 0.6 copy.11
Async XLA Ops:
  0.6 0.8 %copy-start.1 = (bf16[16,128]{1,0:T(8,128)(2,1)S(1)}, bf16[16,128]{1,0:T(8,128)(2,1)}, u32[]{:S(2)}) copy-start(bf16[16,128]{1,0:T(8,128)(2,1)} %points_ref.1) | copy-start | bytes 12292
  0.6 0.8 %copy-start.2 = (f32[128]{0:T(128)S(1)}, f32[128]{0:T(128)}, u32[]{:S(2)}) copy-start(f32[128]{0:T(128)} %param.7) | copy-start | bytes 1540
  0.7 0.8 %copy-start.3 = (f32[16]{0:T(128)S(1)}, f32[16]{0:T(128)}, u32[]{:S(2)}) copy-start(f32[16]{0:T(128)} %scales_ref.1) | copy-start | bytes 196
  1.5 0.8 %copy-start = (f32[64,128]{1,0:T(8,128)S(1)}, f32[64,128]{1,0:T(8,128)}, u32[]{:S(2)}) copy-start(f32[64,128]{1,0:T(8,128)} %right_ref.1) | copy-start | bytes 98308

commit v2 on v1

--- a/solution.py
+++ b/solution.py
@@ -25,7 +25,7 @@
 
 def kernel(
     points_ref, right_ref, nugget_ref, scales_ref, pairs_ref,
-    x_ref, res_ref,
+    out_ref,
     col_pts, row_pts, right_v, nugget_v, scales_s, pairs_s, pen_s,
     inv_v, row_ops, col_ops, tiles,
     v1, v2, p_rows, out1, out2, sib1, sib2, got1, got2, sib_got1, sib_got2, ar,
@@ -57,13 +57,22 @@
     row_to = [device(chip, cc, zhigh + k, xat) for cc in (core, 1 - core) for k in range(4)]
     sum_to = [device(chip, core, zhigh - k, xat) for k in range(4)]
     sibling = device(chip, 1 - core, zhigh, xat)
-    y_line = [device(chip + 2 * k, core, zhigh, xat) for k in range(8)]
-    z_line = [
-        device(chip + dz * (1 - 2 * zlow), core, zhigh + k, xat) for dz in range(2) for k in range(4)
-    ]
-    x_line = [device(chip, cc, zhigh, xat + k) for cc in (core, 1 - core) for k in range(4)]
-
-    greet = col_from[1:] + y_line[1:] + z_line[1:] + x_line[4:] + row_to[5:]
+    y_line = [
+        device(chip + 2 * k, cc, zhigh, xat)
+        for cc, k in [(core, 0)] + [(cc, k) for k in (4, 3, 5, 2, 6, 1, 7, 0) for cc in (1 - core, core)][:-1]
+    ]
+    plane = sorted(
+        ((min(2 * dz, 8 - 2 * dz) + (low if dz < 3 else -low) + min(dx, 4 - dx), dz, low, dx)
+         for dz in range(4) for low in range(2) for dx in range(4)),
+        key=lambda place: -place[0],
+    )
+    plane = plane[-1:] + plane[:-1]
+    plane_line = [
+        device(chip + low * (1 - 2 * zlow), core, zhigh + dz, xat + dx) for _, dz, low, dx in plane
+    ]
+
+    far_y = [device(chip + 8, cc, zhigh, xat) for cc in (core, 1 - core)]
+    greet = far_y + col_from[1:] + row_to[1:]
     barrier = pltpu.get_barrier_semaphore()
     for target in greet:
         pl.semaphore_signal(barrier, inc=1, device_id=target, device_id_type=MESH)
@@ -113,7 +122,7 @@
     inv_v[...] = 1.0 / (inv_v[...] * inv_v[...])
 
     def away(low, offset):
-        value = pairs_s[lax.rem(low + 32, 32), offset - 1]
+        value = pairs_s[offset - 1, lax.rem(low + 32, 32)]
         return (1 - value).astype(F32) * FAR
 
     first = core == 0
@@ -147,24 +156,31 @@
             row_ops[part * FEAT : (part + 1) * FEAT, span] = row_pts[k]
         row_ops[3 * FEAT :, span] = extra.astype(BF16)
 
-    def column(i, chunks):
-        @pl.when(i > 0)
-        def _():
-            remote(col_pts.at[0], col_pts.at[i], pts_send.at[i], pts_recv.at[i], sibling).wait_recv()
-
-        pts = col_pts[i].astype(F32)
-        scaled = split3(pts * (-32.0 * inv_v[...]))
-        one, two, three = norm_rows(pts)
-        extra = jnp.where(at_row == 0, one, 0.0)
-        extra = jnp.where(at_row == 1, two, extra)
-        extra = jnp.where(at_row == 2, three, extra)
-        extra = jnp.where((at_row >= 3) & (at_row < 6), 1.0, extra)
-        extra = jnp.where(at_row == 6, pen_s[i // 4], extra)
-        extra = jnp.where(at_row == 7, pen_s[i // 4 + 4], extra)
-        for part in range(3):
-            col_ops[part * FEAT : (part + 1) * FEAT, :] = scaled[part].astype(BF16)
-        col_ops[3 * FEAT :, :] = extra.astype(BF16)
-        start = pl.multiple_of(i * PIECE, PIECE)
+    def columns_of(j, chunks):
+        for part_at in range(4):
+            i = j * 4 + part_at
+
+            def arrived():
+                remote(col_pts.at[0], col_pts.at[i], pts_send.at[i], pts_recv.at[i], sibling).wait_recv()
+
+            if part_at == 0:
+                pl.when(i > 0)(arrived)
+            else:
+                arrived()
+            pts = col_pts[i].astype(F32)
+            scaled = split3(pts * (-32.0 * inv_v[...]))
+            one, two, three = norm_rows(pts)
+            extra = jnp.where(at_row == 0, one, 0.0)
+            extra = jnp.where(at_row == 1, two, extra)
+            extra = jnp.where(at_row == 2, three, extra)
+            extra = jnp.where((at_row >= 3) & (at_row < 6), 1.0, extra)
+            extra = jnp.where(at_row == 6, pen_s[j], extra)
+            extra = jnp.where(at_row == 7, pen_s[j + 4], extra)
+            at = slice(part_at * PIECE, (part_at + 1) * PIECE)
+            for part in range(3):
+                col_ops[part * FEAT : (part + 1) * FEAT, at] = scaled[part].astype(BF16)
+            col_ops[3 * FEAT :, at] = extra.astype(BF16)
+        start = pl.multiple_of(j * 4 * PIECE, 4 * PIECE)
         ops = col_ops[...]
         for chunk in range(chunks):
             span = slice(chunk * 256, (chunk + 1) * 256)
@@ -174,25 +190,22 @@
             squared = jnp.maximum(squared, 1e-12)
             spare = jnp.maximum(4.0 - squared * lax.rsqrt(squared), 0.0)
             second = spare * spare
-            tiles[pl.ds(start, PIECE), span] = (second * second * (5.0 - spare)).astype(BF16)
-
-    def column_all(i, carry):
-        column(i, 4)
+            tiles[pl.ds(start, 4 * PIECE), span] = (second * second * (5.0 - spare)).astype(BF16)
+
+    def columns_all(j, carry):
+        columns_of(j, 4)
         return carry
 
-    def column_own(i, carry):
-        column(i, 2)
-        return carry
-
-    lax.fori_loop(0, 12, column_all, 0)
-    lax.fori_loop(12, 16, column_own, 0)
-
-    def apply(vec, sib, sib_got, out, got, which):
+    lax.fori_loop(0, 3, columns_all, 0)
+    columns_of(3, 2)
+
+    def apply(vec, sib, sib_got, out, which, between):
         mixed = jnp.dot(vec[:, :1536], tiles[:1536, 512:], preferred_element_type=F32)
         for k in range(4):
             sib[k] = mixed[:, k * PIECE : (k + 1) * PIECE]
         swap = remote(sib, sib_got, sib_send.at[which], sib_recv.at[which], sibling)
         swap.start()
+        between()
         total = jnp.dot(vec[...], tiles[:, :512], preferred_element_type=F32)
         for k in range(4):
             out[k] = total[:, k * PIECE : (k + 1) * PIECE]
@@ -217,7 +230,7 @@
 
     for copy in v1_copies:
         copy.wait_recv()
-    swap1 = apply(v1, sib1, sib_got1, out1, got1, 0)
+    swap1 = apply(v1, sib1, sib_got1, out1, 0, lambda: None)
     sums1 = spread(swap1, sib_got1, out1, got1, 0)
     right = right_v[...]
     nugget = jnp.broadcast_to(nugget_v[...], (NRHS, PIECE))
@@ -230,10 +243,19 @@
         remote(lanes(v2, 0), lanes(v2, i), v2_send.at[i], v2_recv.at[i], col_to[i]) for i in range(1, 16)
     ]
     pr_copies = [
-        remote(lanes(v2, 0), lanes(p_rows, k), pr_send.at[k], pr_recv.at[k], row_to[k]) for k in range(1, 8)
+        remote(lanes(v2, 0), lanes(p_rows, k), pr_send.at[k], pr_recv.at[k], row_to[k]) for k in range(1, 4)
     ]
     for copy in v2_copies + pr_copies:
         copy.start()
+    hand_on = remote(
+        p_rows.at[:, pl.ds(0, 4 * PIECE)], p_rows.at[:, pl.ds(4 * PIECE, 4 * PIECE)],
+        pr_send.at[4], pr_recv.at[4], sibling,
+    )
+
+    def pass_rows():
+        for copy in pr_copies:
+            copy.wait_recv()
+        hand_on.start()
 
     ones = jnp.ones((8, PIECE), F32)
 
@@ -247,9 +269,8 @@
 
     for copy in v2_copies:
         copy.wait_recv()
-    swap2 = apply(v2, sib2, sib_got2, out2, got2, 1)
-    for copy in pr_copies:
-        copy.wait_recv()
+    swap2 = apply(v2, sib2, sib_got2, out2, 1, pass_rows)
+    hand_on.wait_recv()
     form = jnp.zeros((NRHS, PIECE), F32)
     for k in range(4):
         form = form + p_rows[:, k * PIECE : (k + 1) * PIECE].astype(F32) * out2[k]
@@ -258,34 +279,31 @@
     sums_b = across(jnp.concatenate([step_to * step_to, form], axis=0))
     ar[0, 1:2, :] = sums_b[0:1]
 
-    def share(stage, line):
+    def share(base, line):
         copies = [
             remote(
-                ar.at[8 * stage], ar.at[8 * stage + k],
-                ar_send.at[8 * stage + k], ar_recv.at[8 * stage + k], line[k],
+                ar.at[base], ar.at[base + k], ar_send.at[base + k], ar_recv.at[base + k], line[k],
             )
-            for k in range(1, 8)
+            for k in range(1, len(line))
         ]
         for copy in copies:
             copy.start()
         return copies
 
-    def gathered(stage, copies):
+    def gathered(base, copies):
         for copy in copies:
             copy.wait_recv()
-        total = ar[8 * stage]
-        for k in range(1, 8):
-            total = total + ar[8 * stage + k]
-        return total
+        terms = [ar[base + k] for k in range(len(copies) + 1)]
+        while len(terms) > 1:
+            terms = [a + b for a, b in zip(terms[::2], terms[1::2])]
+        return terms[0]
 
     shares_y = share(0, y_line)
     sums2 = spread(swap2, sib_got2, out2, got2, 1)
-    ar[8] = gathered(0, shares_y)
-    shares_x = share(1, x_line)
-    ar[16] = gathered(1, shares_x)
-    shares_z = share(2, z_line)
+    ar[16] = gathered(0, shares_y)
+    shares_plane = share(16, plane_line)
     second_image = nugget * step_to + AMP * collect(sums2, sib_got2, out2, got2)
-    total = gathered(2, shares_z)
+    total = gathered(16, shares_plane)
 
     top, low = total[0:1], total[1:2]
     rr, ru = top, pltpu.roll(top, 64, 1)
@@ -312,39 +330,35 @@
         axis=0,
     )
     columns = coefs.T[:NRHS]
-    x_ref[...] = columns[:, 0:1] * right + columns[:, 1:2] * step_to
-    res_ref[...] = columns[:, 2:3] * right + columns[:, 3:4] * step_to + columns[:, 4:5] * second_image
+    out_ref[:NRHS] = columns[:, 0:1] * right + columns[:, 1:2] * step_to
+    out_ref[NRHS:] = columns[:, 2:3] * right + columns[:, 3:4] * step_to + columns[:, 4:5] * second_image
 
     for copy in (
         row_copies + col_copies + v1_copies + sums1 + v2_copies + pr_copies + sums2
-        + [swap1, swap2] + shares_y + shares_x + shares_z
+        + [swap1, swap2, hand_on] + shares_y + shares_plane
     ):
         copy.wait_send()
 
 
 def on_device(points, right_side, nugget, scales, pairs):
     dma = pltpu.SemaphoreType.DMA
-    any_space = pl.BlockSpec(memory_space=pl.ANY)
-    vmem = pl.BlockSpec(memory_space=pltpu.VMEM)
-    return pl.pallas_call(
+    far_space = pl.BlockSpec(memory_space=pltpu.HBM)
+    both = pl.pallas_call(
         kernel,
-        out_shape=(
-            jax.ShapeDtypeStruct((NRHS, PIECE), F32),
-            jax.ShapeDtypeStruct((NRHS, PIECE), F32),
-        ),
-        in_specs=[any_space] * 5,
-        out_specs=(vmem, vmem),
+        out_shape=jax.ShapeDtypeStruct((2 * NRHS, PIECE), F32),
+        in_specs=[far_space] * 5,
+        out_specs=pl.BlockSpec(memory_space=pltpu.VMEM),
         scratch_shapes=[
             pltpu.VMEM((16, FEAT, PIECE), BF16),
             pltpu.VMEM((8, FEAT, PIECE), BF16),
             pltpu.VMEM((NRHS, PIECE), F32),
             pltpu.VMEM((1, PIECE), F32),
             pltpu.SMEM((FEAT,), F32),
-            pltpu.SMEM((32, 3), jnp.int32),
+            pltpu.SMEM((3, 32), jnp.int32),
             pltpu.SMEM((8,), F32),
             pltpu.VMEM((FEAT, PIECE), F32),
             pltpu.VMEM((4 * FEAT, 8 * PIECE), BF16),
-            pltpu.VMEM((4 * FEAT, PIECE), BF16),
+            pltpu.VMEM((4 * FEAT, 4 * PIECE), BF16),
             pltpu.VMEM((16 * PIECE, 8 * PIECE), BF16),
             pltpu.VMEM((NRHS, 16 * PIECE), BF16),
             pltpu.VMEM((NRHS, 16 * PIECE), BF16),
@@ -352,17 +366,18 @@
         ]
         + [pltpu.VMEM((4, NRHS, PIECE), F32)] * 8
         + [
-            pltpu.VMEM((24, 2, PIECE), F32),
+            pltpu.VMEM((48, 2, PIECE), F32),
             dma((5,)),
             dma((16,)), dma((16,)), dma((8,)), dma((8,)),
             dma((16,)), dma((16,)), dma((16,)), dma((16,)),
             dma((8,)), dma((8,)),
-            dma((2,)), dma((2,)), dma((8,)), dma((8,)), dma((24,)), dma((24,)),
+            dma((2,)), dma((2,)), dma((8,)), dma((8,)), dma((48,)), dma((48,)),
         ],
         compiler_params=pltpu.CompilerParams(
-            collective_id=0, has_side_effects=True, vmem_limit_bytes=40 * 2**20
+            collective_id=0, has_side_effects=True, vmem_limit_bytes=62 * 2**20
         ),
-    )(points, right_side, nugget.reshape(1, PIECE), scales, pairs)
+    )(points, right_side, nugget.reshape(1, PIECE), scales, pairs.T)
+    return both[:NRHS], both[NRHS:]
 
 
 def solution(mesh):

time: 62 us -> 56.8 us (0.916)
  Pallas kernels: 58.3 us -> 54.5 us
  local copies, waits for them, and re-layouts: 2.78 us -> 1.4 us
    pallas_call x1, Pallas kernels: 58.3 us -> 54.5 us  [on_device(): pl.pallas_call(kernel, out_shape=jax.ShapeDtypeStruct((2 * NRHS, PIECE),...]
    unnamed x11 -> x0, local copies, waits for them, and re-layouts: 2.78 us -> none
    slice x0 -> x1, local copies, waits for them, and re-layouts: none -> 1.4 us  [on_device(): return (both[:NRHS], both[NRHS:])]
where the time goes in v2:
time: 56.8 us; the launch traced here: 56.5 us
  Pallas kernels  54.5 us (96%)
  local copies, waits for them, and re-layouts  1.4 us (2%)
  between operations  0.64 us (1%)
    pallas_call x1, Pallas kernels, on_device(): pl.pallas_call(kernel, out_shape=jax.ShapeDtypeStruct((2 * NRHS, PIECE),...  54.5 us
    slice x1, local copies, waits for them, and re-layouts, on_device(): return (both[:NRHS], both[NRHS:])  1.4 us

profile of v2, /device:TPU:1, one launch (start us, length us, event | category | flops | bytes accessed | tf_op | source)
XLA Modules:
  0.0 56.5 jit_solution(13303888704847429761)
XLA Ops:
  0.6 54.5 %shard_map.68 = f32[128,128]{1,0:T(8,128)} custom-call(bf16[16,128]{1,0:T(8,128)(2,1)} %points_ref.1, f32[64,128]{1,0:T(8,128)} %right_ref.1, f32[1,128]{1,0:T(1,128)} %bitcast.3, f32[16]{0:T(128)} %scales_ref.1, s32[3,32]{1,0:T(4,128)} %bitcast.2), custom_call_target="tpu_custom_call" | custom-call | tf_op jit(solution)/shard_map/pallas_call | solution.py:346
  55.1 1.4 %fusion = (f32[64,128]{1,0:T(8,128)}, f32[64,128]{1,0:T(8,128)}) fusion(f32[128,128]{1,0:T(8,128)} %shard_map.68), kind=kLoop, calls=%fused_computation | loop fusion | bytes 131072 | tf_op jit(solution)/shard_map/slice | solution.py:380

commit v3 on v2

--- a/solution.py
+++ b/solution.py
@@ -14,6 +14,10 @@
 NRHS = 64
 FEAT = 16
 AMP = 1.0 / 2064.0 / 256.0
+SHIFTS = (0, 1, 3, 2)
+GROUP = 4 * PIECE
+SIB_GROUP = 3 * PIECE
+FAR_FIRST = [4 * g + j for g in (3, 2, 1, 0) for j in (2, 1, 3, 0)][:-1]
 
 
 def split3(value):
@@ -46,13 +50,13 @@
 
     col_to = [
         device(chip + dm, cc, zhigh, xat + dx)
+        for dx in SHIFTS
         for dm, cc in ((0, core), (side, core), (-side, 1 - core), (-2 * side, 1 - core))
-        for dx in range(4)
     ]
     col_from = [
         device(chip - dm, cc, zhigh, xat - dx)
+        for dx in SHIFTS
         for dm, cc in ((0, core), (side, core), (side, 1 - core), (2 * side, 1 - core))
-        for dx in range(4)
     ]
     row_to = [device(chip, cc, zhigh + k, xat) for cc in (core, 1 - core) for k in range(4)]
     sum_to = [device(chip, core, zhigh - k, xat) for k in range(4)]
@@ -72,7 +76,7 @@
     ]
 
     far_y = [device(chip + 8, cc, zhigh, xat) for cc in (core, 1 - core)]
-    greet = far_y + col_from[1:] + row_to[1:]
+    greet = [col_from[i] for i in FAR_FIRST] + [row_to[k] for k in (2, 6, 1, 3, 5, 7, 4)] + far_y
     barrier = pltpu.get_barrier_semaphore()
     for target in greet:
         pl.semaphore_signal(barrier, inc=1, device_id=target, device_id_type=MESH)
@@ -98,10 +102,11 @@
     loads[0].wait()
     pl.semaphore_wait(barrier, len(greet))
     row_copies = [
-        remote(col_pts.at[0], row_pts.at[k], rpts_send.at[k], rpts_recv.at[k], row_to[k]) for k in range(1, 8)
+        remote(col_pts.at[0], row_pts.at[k], rpts_send.at[k], rpts_recv.at[k], row_to[k])
+        for k in (2, 6, 1, 3, 5, 7, 4)
     ]
     col_copies = [
-        remote(col_pts.at[0], col_pts.at[i], pts_send.at[i], pts_recv.at[i], col_to[i]) for i in range(1, 16)
+        remote(col_pts.at[0], col_pts.at[i], pts_send.at[i], pts_recv.at[i], col_to[i]) for i in FAR_FIRST
     ]
     for copy in row_copies + col_copies:
         copy.start()
@@ -110,7 +115,7 @@
     loads[1].wait()
     v1[:, 0:PIECE] = right_v[...].astype(BF16)
     v1_copies = [
-        remote(lanes(v1, 0), lanes(v1, i), v1_send.at[i], v1_recv.at[i], col_to[i]) for i in range(1, 16)
+        remote(lanes(v1, 0), lanes(v1, i), v1_send.at[i], v1_recv.at[i], col_to[i]) for i in FAR_FIRST
     ]
     for copy in v1_copies:
         copy.start()
@@ -143,7 +148,7 @@
 
     for k in range(8):
         if k:
-            row_copies[k - 1].wait_recv()
+            remote(col_pts.at[0], row_pts.at[k], rpts_send.at[k], rpts_recv.at[k], sibling).wait_recv()
         pts = row_pts[k].astype(F32)
         one, two, three = norm_rows(pts)
         own = at_row == (6 if k < 4 else 7)
@@ -156,14 +161,14 @@
             row_ops[part * FEAT : (part + 1) * FEAT, span] = row_pts[k]
         row_ops[3 * FEAT :, span] = extra.astype(BF16)
 
-    def columns_of(j, chunks):
-        for part_at in range(4):
-            i = j * 4 + part_at
+    def prepare(g):
+        for j in range(4):
+            i = g * 4 + j
 
             def arrived():
                 remote(col_pts.at[0], col_pts.at[i], pts_send.at[i], pts_recv.at[i], sibling).wait_recv()
 
-            if part_at == 0:
+            if j == 0:
                 pl.when(i > 0)(arrived)
             else:
                 arrived()
@@ -176,45 +181,53 @@
             extra = jnp.where((at_row >= 3) & (at_row < 6), 1.0, extra)
             extra = jnp.where(at_row == 6, pen_s[j], extra)
             extra = jnp.where(at_row == 7, pen_s[j + 4], extra)
-            at = slice(part_at * PIECE, (part_at + 1) * PIECE)
+            at = pl.ds(pl.multiple_of(i * PIECE, PIECE), PIECE)
             for part in range(3):
                 col_ops[part * FEAT : (part + 1) * FEAT, at] = scaled[part].astype(BF16)
             col_ops[3 * FEAT :, at] = extra.astype(BF16)
-        start = pl.multiple_of(j * 4 * PIECE, 4 * PIECE)
-        ops = col_ops[...]
-        for chunk in range(chunks):
-            span = slice(chunk * 256, (chunk + 1) * 256)
+
+    def entries(g, depth, first_row):
+        at = pl.ds(pl.multiple_of(g * GROUP, GROUP), depth)
+        ops = col_ops[:, at]
+        for chunk in range(2):
+            span = slice(first_row + chunk * 256, first_row + (chunk + 1) * 256)
             squared = lax.dot_general(
                 ops, row_ops[:, span], (((0,), (0,)), ((), ())), preferred_element_type=F32
             )
             squared = jnp.maximum(squared, 1e-12)
             spare = jnp.maximum(4.0 - squared * lax.rsqrt(squared), 0.0)
             second = spare * spare
-            tiles[pl.ds(start, 4 * PIECE), span] = (second * second * (5.0 - spare)).astype(BF16)
-
-    def columns_all(j, carry):
-        columns_of(j, 4)
+            tiles[at, span] = (second * second * (5.0 - spare)).astype(BF16)
+
+    def near_group(g, carry):
+        prepare(g)
+        entries(g, SIB_GROUP, 512)
+        entries(g, GROUP, 0)
         return carry
 
-    lax.fori_loop(0, 3, columns_all, 0)
-    columns_of(3, 2)
-
-    def apply(vec, sib, sib_got, out, which, between):
-        mixed = jnp.dot(vec[:, :1536], tiles[:1536, 512:], preferred_element_type=F32)
-        for k in range(4):
-            sib[k] = mixed[:, k * PIECE : (k + 1) * PIECE]
-        swap = remote(sib, sib_got, sib_send.at[which], sib_recv.at[which], sibling)
-        swap.start()
-        between()
-        total = jnp.dot(vec[...], tiles[:, :512], preferred_element_type=F32)
-        for k in range(4):
-            out[k] = total[:, k * PIECE : (k + 1) * PIECE]
-        return swap
-
-    def spread(swap, sib_got, out, got, which):
-        swap.wait_recv()
+    def far_group(g, carry):
+        prepare(g)
+        entries(g, SIB_GROUP, 512)
+        return carry
+
+    def far_group_own(g, carry):
+        entries(g, GROUP, 0)
+        return carry
+
+    def sib_part(vec, g):
+        return jnp.dot(
+            vec[:, g * GROUP : g * GROUP + SIB_GROUP],
+            tiles[g * GROUP : g * GROUP + SIB_GROUP, 512:],
+            preferred_element_type=F32,
+        )
+
+    def pieces(ref, values, first):
+        for k in range(values.shape[1] // PIECE):
+            ref[first + k] = values[:, k * PIECE : (k + 1) * PIECE]
+
+    def spread(sib_got, out, got, which, order):
         copies = []
-        for k in (2, 1, 3):
+        for k in order:
             out[k] = out[k] + sib_got[k]
             copies.append(
                 remote(out.at[k], got.at[k], rs_send.at[4 * which + k], rs_recv.at[4 * which + k], sum_to[k])
@@ -228,10 +241,21 @@
             copy.wait_recv()
         return mine + got[1] + got[2] + got[3]
 
+    swap1 = remote(sib1, sib_got1, sib_send.at[0], sib_recv.at[0], sibling)
+    swap2 = remote(sib2, sib_got2, sib_send.at[1], sib_recv.at[1], sibling)
+
+    lax.fori_loop(0, 2, near_group, 0)
+    lax.fori_loop(2, 4, far_group, 0)
     for copy in v1_copies:
         copy.wait_recv()
-    swap1 = apply(v1, sib1, sib_got1, out1, 0, lambda: None)
-    sums1 = spread(swap1, sib_got1, out1, got1, 0)
+    pieces(sib1, sib_part(v1, 0) + sib_part(v1, 1) + sib_part(v1, 2) + sib_part(v1, 3), 0)
+    swap1.start()
+    lax.fori_loop(2, 4, far_group_own, 0)
+    pieces(out1, jnp.dot(v1[...], tiles[:, 256:512], preferred_element_type=F32), 2)
+    swap1.wait_recv()
+    sums1 = spread(sib_got1, out1, got1, 0, (2, 3))
+    pieces(out1, jnp.dot(v1[...], tiles[:, :256], preferred_element_type=F32), 0)
+    sums1 = sums1 + spread(sib_got1, out1, got1, 0, (1,))
     right = right_v[...]
     nugget = jnp.broadcast_to(nugget_v[...], (NRHS, PIECE))
     image = nugget * right + AMP * collect(sums1, sib_got1, out1, got1)
@@ -240,10 +264,10 @@
     v2[:, 0:PIECE] = rounded
     p_rows[:, 0:PIECE] = rounded
     v2_copies = [
-        remote(lanes(v2, 0), lanes(v2, i), v2_send.at[i], v2_recv.at[i], col_to[i]) for i in range(1, 16)
+        remote(lanes(v2, 0), lanes(v2, i), v2_send.at[i], v2_recv.at[i], col_to[i]) for i in FAR_FIRST
     ]
     pr_copies = [
-        remote(lanes(v2, 0), lanes(p_rows, k), pr_send.at[k], pr_recv.at[k], row_to[k]) for k in range(1, 4)
+        remote(lanes(v2, 0), lanes(p_rows, k), pr_send.at[k], pr_recv.at[k], row_to[k]) for k in (2, 1, 3)
     ]
     for copy in v2_copies + pr_copies:
         copy.start()
@@ -252,11 +276,6 @@
         pr_send.at[4], pr_recv.at[4], sibling,
     )
 
-    def pass_rows():
-        for copy in pr_copies:
-            copy.wait_recv()
-        hand_on.start()
-
     ones = jnp.ones((8, PIECE), F32)
 
     def across(values):
@@ -267,13 +286,29 @@
     sums_a = across(jnp.concatenate([right * right, right * image], axis=0))
     ar[0, 0:1, :] = sums_a[0:1]
 
-    for copy in v2_copies:
-        copy.wait_recv()
-    swap2 = apply(v2, sib2, sib_got2, out2, 1, pass_rows)
-    hand_on.wait_recv()
+    mixed = jnp.zeros((NRHS, 4 * PIECE), F32)
+    total = jnp.zeros((NRHS, 4 * PIECE), F32)
+    for g in range(4):
+        for copy, i in zip(v2_copies, FAR_FIRST):
+            if i // 4 == g:
+                copy.wait_recv()
+        mixed = mixed + sib_part(v2, g)
+        if g == 3:
+            for copy in pr_copies:
+                copy.wait_recv()
+            hand_on.start()
+        total = total + jnp.dot(
+            v2[:, g * GROUP : (g + 1) * GROUP],
+            tiles[g * GROUP : (g + 1) * GROUP, :512],
+            preferred_element_type=F32,
+        )
+    pieces(sib2, mixed, 0)
+    pieces(out2, total, 0)
     form = jnp.zeros((NRHS, PIECE), F32)
     for k in range(4):
         form = form + p_rows[:, k * PIECE : (k + 1) * PIECE].astype(F32) * out2[k]
+    hand_on.wait_recv()
+    for k in range(4):
         form = form + p_rows[:, (k + 4) * PIECE : (k + 5) * PIECE].astype(F32) * sib2[k]
     form = nugget * step_to * step_to + AMP * form
     sums_b = across(jnp.concatenate([step_to * step_to, form], axis=0))
@@ -299,7 +334,9 @@
         return terms[0]
 
     shares_y = share(0, y_line)
-    sums2 = spread(swap2, sib_got2, out2, got2, 1)
+    swap2.start()
+    swap2.wait_recv()
+    sums2 = spread(sib_got2, out2, got2, 1, (2, 1, 3))
     ar[16] = gathered(0, shares_y)
     shares_plane = share(16, plane_line)
     second_image = nugget * step_to + AMP * collect(sums2, sib_got2, out2, got2)
@@ -342,6 +379,8 @@
 
 def on_device(points, right_side, nugget, scales, pairs):
     dma = pltpu.SemaphoreType.DMA
+    operands = (points, right_side, nugget.reshape(1, PIECE), scales, pairs.T)
+    operands = [pltpu.with_memory_space_constraint(array, pltpu.HBM) for array in operands]
     far_space = pl.BlockSpec(memory_space=pltpu.HBM)
     both = pl.pallas_call(
         kernel,
@@ -358,7 +397,7 @@
             pltpu.SMEM((8,), F32),
             pltpu.VMEM((FEAT, PIECE), F32),
             pltpu.VMEM((4 * FEAT, 8 * PIECE), BF16),
-            pltpu.VMEM((4 * FEAT, 4 * PIECE), BF16),
+            pltpu.VMEM((4 * FEAT, 16 * PIECE), BF16),
             pltpu.VMEM((16 * PIECE, 8 * PIECE), BF16),
             pltpu.VMEM((NRHS, 16 * PIECE), BF16),
             pltpu.VMEM((NRHS, 16 * PIECE), BF16),
@@ -374,9 +413,9 @@
             dma((2,)), dma((2,)), dma((8,)), dma((8,)), dma((48,)), dma((48,)),
         ],
         compiler_params=pltpu.CompilerParams(
-            collective_id=0, has_side_effects=True, vmem_limit_bytes=62 * 2**20
+            collective_id=0, has_side_effects=True, vmem_limit_bytes=40 * 2**20
         ),
-    )(points, right_side, nugget.reshape(1, PIECE), scales, pairs.T)
+    )(*operands)
     return both[:NRHS], both[NRHS:]
 
 

time: 56.8 us -> 53.5 us (0.942)
  Pallas kernels: 54.5 us -> 52.1 us
  local copies, waits for them, and re-layouts: 1.4 us -> 0.63 us
    pallas_call x1, Pallas kernels: 54.5 us -> 52.1 us  [on_device(): pl.pallas_call(kernel, out_shape=jax.ShapeDtypeStruct((2 * NRHS, PIECE),...]
    slice x1, local copies, waits for them, and re-layouts: 1.4 us -> 0.63 us  [on_device(): return (both[:NRHS], both[NRHS:])]
where the time goes in v3:
time: 53.5 us; the launch traced here: 53.3 us
  Pallas kernels  52.1 us (97%)
  between operations  0.64 us (1%)
  local copies, waits for them, and re-layouts  0.63 us (1%)
    pallas_call x1, Pallas kernels, on_device(): pl.pallas_call(kernel, out_shape=jax.ShapeDtypeStruct((2 * NRHS, PIECE),...  52.1 us

profile of v3, /device:TPU:1, one launch (start us, length us, event | category | flops | bytes accessed | tf_op | source)
XLA Modules:
  0.0 53.3 jit_solution(18110875539793720089)
XLA Ops:
  0.6 52.1 %shard_map.68 = f32[128,128]{1,0:T(8,128)S(1)} custom-call(bf16[16,128]{1,0:T(8,128)(2,1)} %points_ref.1, f32[64,128]{1,0:T(8,128)} %right_ref.1, f32[1,128]{1,0:T(1,128)} %bitcast.3, f32[16]{0:T(128)} %scales_ref.1, s32[3,32]{1,0:T(4,128)} %bitcast.2), custom_call_target="tpu_custom_call" | custom-call | tf_op jit(solution)/shard_map/pallas_call | solution.py:385
  52.7 0.6 %fusion = (f32[64,128]{1,0:T(8,128)}, f32[64,128]{1,0:T(8,128)}) fusion(f32[128,128]{1,0:T(8,128)S(1)} %shard_map.68), kind=kLoop, calls=%fused_computation | loop fusion | bytes 131072 | tf_op jit(solution)/shard_map/slice | solution.py:419

commit v4 on v3

--- a/solution.py
+++ b/solution.py
@@ -32,7 +32,7 @@
     out_ref,
     col_pts, row_pts, right_v, nugget_v, scales_s, pairs_s, pen_s,
     inv_v, row_ops, col_ops, tiles,
-    v1, v2, p_rows, out1, out2, sib1, sib2, got1, got2, sib_got1, sib_got2, ar,
+    v1, v2, v1_slots, v2_slots, p_rows, out1, out2, sib1, sib2, got1, got2, sib_got1, sib_got2, ar,
     local_sem, pts_send, pts_recv, rpts_send, rpts_recv, v1_send, v1_recv, v2_send, v2_recv,
     pr_send, pr_recv, sib_send, sib_recv, rs_send, rs_recv, ar_send, ar_recv,
 ):
@@ -96,8 +96,9 @@
             src_ref=src, dst_ref=dst, send_sem=send, recv_sem=recv, device_id=target, device_id_type=MESH
         )
 
-    def lanes(ref, index):
-        return ref.at[:, pl.ds(index * PIECE, PIECE)]
+    def lay_out(vec, slots, first, last):
+        for i in range(first, last):
+            vec[:, i * PIECE : (i + 1) * PIECE] = slots[i]
 
     loads[0].wait()
     pl.semaphore_wait(barrier, len(greet))
@@ -113,9 +114,9 @@
     row_pts[0] = col_pts[0]
 
     loads[1].wait()
-    v1[:, 0:PIECE] = right_v[...].astype(BF16)
+    v1_slots[0] = right_v[...].astype(BF16)
     v1_copies = [
-        remote(lanes(v1, 0), lanes(v1, i), v1_send.at[i], v1_recv.at[i], col_to[i]) for i in FAR_FIRST
+        remote(v1_slots.at[0], v1_slots.at[i], v1_send.at[i], v1_recv.at[i], col_to[i]) for i in FAR_FIRST
     ]
     for copy in v1_copies:
         copy.start()
@@ -186,32 +187,30 @@
                 col_ops[part * FEAT : (part + 1) * FEAT, at] = scaled[part].astype(BF16)
             col_ops[3 * FEAT :, at] = extra.astype(BF16)
 
-    def entries(g, depth, first_row):
-        at = pl.ds(pl.multiple_of(g * GROUP, GROUP), depth)
-        ops = col_ops[:, at]
-        for chunk in range(2):
-            span = slice(first_row + chunk * 256, first_row + (chunk + 1) * 256)
-            squared = lax.dot_general(
-                ops, row_ops[:, span], (((0,), (0,)), ((), ())), preferred_element_type=F32
-            )
-            squared = jnp.maximum(squared, 1e-12)
-            spare = jnp.maximum(4.0 - squared * lax.rsqrt(squared), 0.0)
-            second = spare * spare
-            tiles[at, span] = (second * second * (5.0 - spare)).astype(BF16)
-
-    def near_group(g, carry):
+    def entries(start, depth, first_row):
+        at = pl.ds(start, depth)
+        span = slice(first_row, first_row + 256)
+        squared = lax.dot_general(
+            col_ops[:, at], row_ops[:, span], (((0,), (0,)), ((), ())), preferred_element_type=F32
+        )
+        squared = jnp.maximum(squared, 1e-12)
+        spare = jnp.maximum(4.0 - squared * lax.rsqrt(squared), 0.0)
+        second = spare * spare
+        tiles[at, span] = (second * second * (5.0 - spare)).astype(BF16)
+
+    def sib_group(g, carry):
         prepare(g)
-        entries(g, SIB_GROUP, 512)
-        entries(g, GROUP, 0)
+        start = pl.multiple_of(g * GROUP, GROUP)
+        entries(start, SIB_GROUP, 512)
+        entries(start, SIB_GROUP, 768)
         return carry
 
-    def far_group(g, carry):
-        prepare(g)
-        entries(g, SIB_GROUP, 512)
+    def own_high(h, carry):
+        entries(pl.multiple_of(h * 2 * GROUP, 2 * GROUP), 2 * GROUP, 256)
         return carry
 
-    def far_group_own(g, carry):
-        entries(g, GROUP, 0)
+    def own_low(h, carry):
+        entries(pl.multiple_of(h * 2 * GROUP, 2 * GROUP), 2 * GROUP, 0)
         return carry
 
     def sib_part(vec, g):
@@ -244,16 +243,17 @@
     swap1 = remote(sib1, sib_got1, sib_send.at[0], sib_recv.at[0], sibling)
     swap2 = remote(sib2, sib_got2, sib_send.at[1], sib_recv.at[1], sibling)
 
-    lax.fori_loop(0, 2, near_group, 0)
-    lax.fori_loop(2, 4, far_group, 0)
+    lax.fori_loop(0, 4, sib_group, 0)
     for copy in v1_copies:
         copy.wait_recv()
+    lay_out(v1, v1_slots, 0, 16)
     pieces(sib1, sib_part(v1, 0) + sib_part(v1, 1) + sib_part(v1, 2) + sib_part(v1, 3), 0)
     swap1.start()
-    lax.fori_loop(2, 4, far_group_own, 0)
+    lax.fori_loop(0, 2, own_high, 0)
     pieces(out1, jnp.dot(v1[...], tiles[:, 256:512], preferred_element_type=F32), 2)
     swap1.wait_recv()
     sums1 = spread(sib_got1, out1, got1, 0, (2, 3))
+    lax.fori_loop(0, 2, own_low, 0)
     pieces(out1, jnp.dot(v1[...], tiles[:, :256], preferred_element_type=F32), 0)
     sums1 = sums1 + spread(sib_got1, out1, got1, 0, (1,))
     right = right_v[...]
@@ -261,18 +261,18 @@
     image = nugget * right + AMP * collect(sums1, sib_got1, out1, got1)
     step_to = right - STEP * image
     rounded = step_to.astype(BF16)
-    v2[:, 0:PIECE] = rounded
-    p_rows[:, 0:PIECE] = rounded
+    v2_slots[0] = rounded
+    p_rows[0] = rounded
     v2_copies = [
-        remote(lanes(v2, 0), lanes(v2, i), v2_send.at[i], v2_recv.at[i], col_to[i]) for i in FAR_FIRST
+        remote(v2_slots.at[0], v2_slots.at[i], v2_send.at[i], v2_recv.at[i], col_to[i]) for i in FAR_FIRST
     ]
     pr_copies = [
-        remote(lanes(v2, 0), lanes(p_rows, k), pr_send.at[k], pr_recv.at[k], row_to[k]) for k in (2, 1, 3)
-    ]
-    for copy in v2_copies + pr_copies:
+        remote(v2_slots.at[0], p_rows.at[k], pr_send.at[k], pr_recv.at[k], row_to[k]) for k in (2, 1, 3)
+    ]
+    for copy in pr_copies + v2_copies:
         copy.start()
     hand_on = remote(
-        p_rows.at[:, pl.ds(0, 4 * PIECE)], p_rows.at[:, pl.ds(4 * PIECE, 4 * PIECE)],
+        p_rows.at[pl.ds(0, 4)], p_rows.at[pl.ds(4, 4)],
         pr_send.at[4], pr_recv.at[4], sibling,
     )
 
@@ -292,6 +292,7 @@
         for copy, i in zip(v2_copies, FAR_FIRST):
             if i // 4 == g:
                 copy.wait_recv()
+        lay_out(v2, v2_slots, 4 * g, 4 * g + 4)
         mixed = mixed + sib_part(v2, g)
         if g == 3:
             for copy in pr_copies:
@@ -306,10 +307,10 @@
     pieces(out2, total, 0)
     form = jnp.zeros((NRHS, PIECE), F32)
     for k in range(4):
-        form = form + p_rows[:, k * PIECE : (k + 1) * PIECE].astype(F32) * out2[k]
+        form = form + p_rows[k].astype(F32) * out2[k]
     hand_on.wait_recv()
     for k in range(4):
-        form = form + p_rows[:, (k + 4) * PIECE : (k + 5) * PIECE].astype(F32) * sib2[k]
+        form = form + p_rows[k + 4].astype(F32) * sib2[k]
     form = nugget * step_to * step_to + AMP * form
     sums_b = across(jnp.concatenate([step_to * step_to, form], axis=0))
     ar[0, 1:2, :] = sums_b[0:1]
@@ -401,7 +402,9 @@
             pltpu.VMEM((16 * PIECE, 8 * PIECE), BF16),
             pltpu.VMEM((NRHS, 16 * PIECE), BF16),
             pltpu.VMEM((NRHS, 16 * PIECE), BF16),
-            pltpu.VMEM((NRHS, 8 * PIECE), BF16),
+            pltpu.VMEM((16, NRHS, PIECE), BF16),
+            pltpu.VMEM((16, NRHS, PIECE), BF16),
+            pltpu.VMEM((8, NRHS, PIECE), BF16),
         ]
         + [pltpu.VMEM((4, NRHS, PIECE), F32)] * 8
         + [

time: 53.5 us -> 52.4 us (0.979)
  Pallas kernels: 52.1 us -> 50.9 us
    pallas_call x1, Pallas kernels: 52.1 us -> 50.9 us  [on_device(): pl.pallas_call(kernel, out_shape=jax.ShapeDtypeStruct((2 * NRHS, PIECE),...]
where the time goes in v4:
time: 52.4 us; the launch traced here: 52.2 us
  Pallas kernels  50.9 us (97%)
  between operations  0.64 us (1%)
  local copies, waits for them, and re-layouts  0.63 us (1%)
    pallas_call x1, Pallas kernels, on_device(): pl.pallas_call(kernel, out_shape=jax.ShapeDtypeStruct((2 * NRHS, PIECE),...  50.9 us

profile of v4, /device:TPU:1, one launch (start us, length us, event | category | flops | bytes accessed | tf_op | source)
XLA Modules:
  0.0 52.2 jit_solution(17521832042605159767)
XLA Ops:
  0.6 50.9 %shard_map.68 = f32[128,128]{1,0:T(8,128)S(1)} custom-call(bf16[16,128]{1,0:T(8,128)(2,1)} %points_ref.1, f32[64,128]{1,0:T(8,128)} %right_ref.1, f32[1,128]{1,0:T(1,128)} %bitcast.3, f32[16]{0:T(128)} %scales_ref.1, s32[3,32]{1,0:T(4,128)} %bitcast.2), custom_call_target="tpu_custom_call" | custom-call | tf_op jit(solution)/shard_map/pallas_call | solution.py:386
  51.6 0.6 %fusion = (f32[64,128]{1,0:T(8,128)}, f32[64,128]{1,0:T(8,128)}) fusion(f32[128,128]{1,0:T(8,128)S(1)} %shard_map.68), kind=kLoop, calls=%fused_computation | loop fusion | bytes 131072 | tf_op jit(solution)/shard_map/slice | solution.py:422

commit v5 on v4

--- a/solution.py
+++ b/solution.py
@@ -266,14 +266,21 @@
     v2_copies = [
         remote(v2_slots.at[0], v2_slots.at[i], v2_send.at[i], v2_recv.at[i], col_to[i]) for i in FAR_FIRST
     ]
-    pr_copies = [
-        remote(v2_slots.at[0], p_rows.at[k], pr_send.at[k], pr_recv.at[k], row_to[k]) for k in (2, 1, 3)
-    ]
-    for copy in pr_copies + v2_copies:
+    across_z, next_z, twin = (
+        remote(v2_slots.at[0], p_rows.at[k], pr_send.at[k], pr_recv.at[k], target)
+        for k, target in ((2, row_to[2]), (3, row_to[1]), (4, sibling))
+    )
+    upper = zhigh >= 2
+
+    @pl.when(upper)
+    def _():
+        across_z.start()
+        p_rows[2] = jnp.zeros((NRHS, PIECE), BF16)
+
+    for copy in [next_z] + v2_copies + [twin]:
         copy.start()
     hand_on = remote(
-        p_rows.at[pl.ds(0, 4)], p_rows.at[pl.ds(4, 4)],
-        pr_send.at[4], pr_recv.at[4], sibling,
+        p_rows.at[pl.ds(2, 2)], p_rows.at[pl.ds(6, 2)], pr_send.at[5], pr_recv.at[5], sibling
     )
 
     ones = jnp.ones((8, PIECE), F32)
@@ -295,8 +302,8 @@
         lay_out(v2, v2_slots, 4 * g, 4 * g + 4)
         mixed = mixed + sib_part(v2, g)
         if g == 3:
-            for copy in pr_copies:
-                copy.wait_recv()
+            next_z.wait_recv()
+            pl.when(zhigh < 2)(across_z.wait_recv)
             hand_on.start()
         total = total + jnp.dot(
             v2[:, g * GROUP : (g + 1) * GROUP],
@@ -305,12 +312,12 @@
         )
     pieces(sib2, mixed, 0)
     pieces(out2, total, 0)
-    form = jnp.zeros((NRHS, PIECE), F32)
-    for k in range(4):
-        form = form + p_rows[k].astype(F32) * out2[k]
+    form = 2.0 * (p_rows[2].astype(F32) * out2[2] + p_rows[3].astype(F32) * out2[1])
+    form = form + p_rows[0].astype(F32) * out2[0]
+    twin.wait_recv()
+    form = form + p_rows[4].astype(F32) * sib2[0]
     hand_on.wait_recv()
-    for k in range(4):
-        form = form + p_rows[k + 4].astype(F32) * sib2[k]
+    form = form + 2.0 * (p_rows[6].astype(F32) * sib2[2] + p_rows[7].astype(F32) * sib2[1])
     form = nugget * step_to * step_to + AMP * form
     sums_b = across(jnp.concatenate([step_to * step_to, form], axis=0))
     ar[0, 1:2, :] = sums_b[0:1]
@@ -372,10 +379,11 @@
     out_ref[NRHS:] = columns[:, 2:3] * right + columns[:, 3:4] * step_to + columns[:, 4:5] * second_image
 
     for copy in (
-        row_copies + col_copies + v1_copies + sums1 + v2_copies + pr_copies + sums2
+        row_copies + col_copies + v1_copies + sums1 + v2_copies + [next_z, twin] + sums2
         + [swap1, swap2, hand_on] + shares_y + shares_plane
     ):
         copy.wait_send()
+    pl.when(upper)(across_z.wait_send)
 
 
 def on_device(points, right_side, nugget, scales, pairs):

time: 52.4 us -> 51.7 us (0.987)
  Pallas kernels: 50.9 us -> 50.2 us
    pallas_call x1, Pallas kernels: 50.9 us -> 50.2 us  [on_device(): pl.pallas_call(kernel, out_shape=jax.ShapeDtypeStruct((2 * NRHS, PIECE),...]
where the time goes in v5:
time: 51.7 us; the launch traced here: 51.5 us
  Pallas kernels  50.2 us (97%)
  between operations  0.64 us (1%)
  local copies, waits for them, and re-layouts  0.63 us (1%)
    pallas_call x1, Pallas kernels, on_device(): pl.pallas_call(kernel, out_shape=jax.ShapeDtypeStruct((2 * NRHS, PIECE),...  50.2 us

profile of v5, /device:TPU:1, one launch (start us, length us, event | category | flops | bytes accessed | tf_op | source)
XLA Modules:
  0.0 51.5 jit_solution(6068251873146850757)
XLA Ops:
  0.6 50.2 %shard_map.68 = f32[128,128]{1,0:T(8,128)S(1)} custom-call(bf16[16,128]{1,0:T(8,128)(2,1)} %points_ref.1, f32[64,128]{1,0:T(8,128)} %right_ref.1, f32[1,128]{1,0:T(1,128)} %bitcast.3, f32[16]{0:T(128)} %scales_ref.1, s32[3,32]{1,0:T(4,128)} %bitcast.2), custom_call_target="tpu_custom_call" | custom-call | tf_op jit(solution)/shard_map/pallas_call | solution.py:394
  50.9 0.6 %fusion = (f32[64,128]{1,0:T(8,128)}, f32[64,128]{1,0:T(8,128)}) fusion(f32[128,128]{1,0:T(8,128)S(1)} %shard_map.68), kind=kLoop, calls=%fused_computation | loop fusion | bytes 131072 | tf_op jit(solution)/shard_map/slice | solution.py:430
